TPU v7x, 512 devices: a whole 4x4x16 slice. The times are simulated.
512 devices in a mesh: dp: 16 (over z), head: 8 (over x, core), srv: 4 (over y).
Axes of the slice: x: 4, y: 4, z: 16, core: 2. Of those that a mesh axis runs over, the one named last changes fastest.
Arguments:
- queries: bfloat16 [2048, 8, 1024], P('dp', 'srv', 'head'), may hold values from -5 to 5
- keys: bfloat16 [10240, 1024], P(('dp', 'head')), may hold values from -5 to 5
- values: bfloat16 [10240, 1024], P(('dp', 'head')), may hold values from -6 to 6
- output_gradient: bfloat16 [2048, 8, 1024], P('dp', 'srv', 'head'), may hold values from -6 to 6
- doc_ids: int32 [10240], P('dp'), may hold values from 0 to 7, never falling along the last dimension, each value on 1 to 5120 neighbouring positions
Outputs:
- attention: bfloat16 [2048, 8, 1024], P('dp', 'srv', 'head')
- q_grad: bfloat16 [2048, 8, 1024], P('dp', 'srv', 'head')
- k_grad: bfloat16 [10240, 1024], P(('dp', 'head', 'srv'))
- v_grad: bfloat16 [10240, 1024], P(('dp', 'head', 'srv'))
Inputs may be any that keep to these rules, and one draw needn't show every extreme that they name: `doc_ids`: document numbers never fall along the keys; every document holds at most 5120 keys, and one holds exactly 5120.
All inputs are finite; a program needn't handle non-finite values.
Results may differ from a plain program's by a relative error of at most 0.039.
Values may be sent and summed in bfloat16 or wider, within the bound.
No kernel may reach another device: no remote copies, remote signals or barrier semaphores. Data moves between devices by JAX's collectives and lax.ppermute only.
A program may use at most 64 MiB of HBM per device.

v0:
```python
import math
import jax
import jax.numpy as jnp
from jax import lax
from jax.sharding import PartitionSpec as P

HEAD_SIZE = 128
NEGATIVE = -1e30


def local(queries, keys, values, output_gradient, doc_ids):
    home_rows, pair_heads, group_width = queries.shape
    groups = group_width // HEAD_SIZE
    scale_factor = HEAD_SIZE ** (-0.5)
    key_rows, value_rows = (
        lax.all_to_all(keys, "head", split_axis=1, concat_axis=0, tiled=True),
        lax.all_to_all(values, "head", split_axis=1, concat_axis=0, tiled=True),
    )
    key_count = key_rows.shape[0]
    servers = lax.axis_size("dp")
    server = lax.axis_index("dp")
    key_at = server * key_count + jnp.arange(key_count, dtype=jnp.int32)
    all_docs = lax.all_gather(doc_ids, "dp", axis=0, tiled=True)
    query_total = home_rows * servers
    context = all_docs.shape[0] - query_total
    query_docs = all_docs[context:]
    query_places = context + jnp.arange(query_total, dtype=jnp.int32)
    all_q, all_dout = (
        lax.all_gather(queries, "dp", axis=0, tiled=True),
        lax.all_gather(output_gradient, "dp", axis=0, tiled=True),
    )
    block_rows = math.gcd(512, query_total)
    block_count = query_total // block_rows
    key_heads = key_rows.reshape(key_count, groups, HEAD_SIZE)
    value_heads = value_rows.reshape(key_count, groups, HEAD_SIZE)
    query_blocks = all_q.reshape(block_count, block_rows, pair_heads, groups, HEAD_SIZE)
    grad_blocks = all_dout.reshape(block_count, block_rows, pair_heads, groups, HEAD_SIZE)
    place_blocks = query_places.reshape(block_count, block_rows)
    doc_blocks = query_docs.reshape(block_count, block_rows)

    def admissible(places, query_doc):
        return (key_at[None, :] <= places[:, None]) & (doc_ids[None, :] == query_doc[:, None])

    def scores_of(query_block):
        return (
            jnp.einsum("pjgd,kgd->gjpk", query_block, key_heads, preferred_element_type=jnp.float32)
            * scale_factor
        )

    def block_max(inputs):
        query_block, places, query_doc = inputs
        allowed = admissible(places, query_doc)

        def compute():
            raw_scores = scores_of(query_block)
            masked = jnp.where(allowed[None, None], raw_scores, NEGATIVE)
            return (jnp.max(masked, axis=-1).transpose(2, 1, 0), raw_scores)

        return compute()

    def block_top(inputs):
        return block_max(inputs)[0]

    local_max = lax.map(block_top, (query_blocks, place_blocks, doc_blocks))
    row_max = lax.pmax(local_max.reshape(query_total, pair_heads, groups), "dp")
    max_blocks = row_max.reshape(block_count, block_rows, pair_heads, groups)

    def block_sum(inputs):
        stored, places, query_doc, row_top = inputs
        allowed = admissible(places, query_doc)

        def compute():
            block_scores = scores_of(stored)
            shifted = block_scores - row_top.transpose(2, 1, 0)[..., None]
            weights = jnp.where(allowed[None, None], jnp.exp(shifted), 0.0)
            weighted = jnp.einsum(
                "gjpk,kgd->pjgd",
                weights.astype(jnp.bfloat16),
                value_heads,
                preferred_element_type=jnp.float32,
            )
            return (
                weighted.reshape(block_rows, pair_heads, group_width),
                jnp.sum(weights, axis=-1).transpose(2, 1, 0),
            )

        return compute()

    part_out, part_norm = lax.map(block_sum, (query_blocks, place_blocks, doc_blocks, max_blocks))
    part_out = part_out.reshape(query_total, pair_heads, group_width)
    part_norm = part_norm.reshape(query_total, pair_heads, groups)
    home_out, home_norm = (
        lax.psum_scatter(part_out, "dp", scatter_dimension=0, tiled=True),
        lax.psum_scatter(part_norm, "dp", scatter_dimension=0, tiled=True),
    )
    home_max = lax.dynamic_slice_in_dim(row_max, server * home_rows, home_rows, 0)
    attn_home = (
        home_out.reshape(home_rows, pair_heads, groups, HEAD_SIZE) / home_norm[..., None]
    ).astype(jnp.bfloat16)
    log_home = home_max + jnp.log(home_norm)
    grad_home = output_gradient.reshape(home_rows, pair_heads, groups, HEAD_SIZE).astype(
        jnp.float32
    )
    delta_home = jnp.sum(grad_home * attn_home.astype(jnp.float32), axis=-1)
    log_all, delta_all = (
        lax.all_gather(log_home, "dp", axis=0, tiled=True),
        lax.all_gather(delta_home, "dp", axis=0, tiled=True),
    )
    attention = attn_home.reshape(home_rows, pair_heads, group_width)
    log_blocks = log_all.reshape(block_count, block_rows, pair_heads, groups)
    delta_blocks = delta_all.reshape(block_count, block_rows, pair_heads, groups)

    def block_grad(totals, inputs):
        query_block, grad_block, places, query_doc, log_norm, row_delta = inputs
        allowed = admissible(places, query_doc)

        def compute():
            shifted = scores_of(query_block) - log_norm.transpose(2, 1, 0)[..., None]
            probs = jnp.where(allowed[None, None], jnp.exp(shifted), 0.0)
            value_grad = jnp.einsum(
                "gjpk,pjgd->kgd",
                probs.astype(jnp.bfloat16),
                grad_block,
                preferred_element_type=jnp.float32,
            )
            weight_grad = jnp.einsum(
                "pjgd,kgd->gjpk", grad_block, value_heads, preferred_element_type=jnp.float32
            )
            score_grad = (probs * (weight_grad - row_delta.transpose(2, 1, 0)[..., None])).astype(
                jnp.bfloat16
            )
            query_grad = (
                jnp.einsum(
                    "gjpk,kgd->pjgd", score_grad, key_heads, preferred_element_type=jnp.float32
                )
                * scale_factor
            )
            key_grad = (
                jnp.einsum(
                    "gjpk,pjgd->kgd", score_grad, query_block, preferred_element_type=jnp.float32
                )
                * scale_factor
            )
            return (query_grad.reshape(block_rows, pair_heads, group_width), key_grad, value_grad)

        query_grad, key_grad, value_grad = compute()
        return ((totals[0] + key_grad, totals[1] + value_grad), query_grad)

    zero_start = jnp.zeros((key_count, groups, HEAD_SIZE), jnp.float32)
    grad_inputs = (query_blocks, grad_blocks, place_blocks, doc_blocks, log_blocks, delta_blocks)
    (key_total, value_total), query_parts = lax.scan(
        block_grad, (zero_start, zero_start), grad_inputs
    )
    q_summed = lax.psum_scatter(
        query_parts.reshape(query_total, pair_heads, group_width).astype(jnp.bfloat16),
        "dp",
        scatter_dimension=0,
        tiled=True,
    )
    spread_key, spread_value = (
        lax.all_to_all(
            key_total.reshape(key_count, group_width).astype(jnp.bfloat16),
            "head",
            split_axis=0,
            concat_axis=1,
            tiled=True,
        ).astype(jnp.float32),
        lax.all_to_all(
            value_total.reshape(key_count, group_width).astype(jnp.bfloat16),
            "head",
            split_axis=0,
            concat_axis=1,
            tiled=True,
        ).astype(jnp.float32),
    )
    k_summed, v_summed = (
        lax.psum_scatter(
            spread_key.astype(jnp.bfloat16), "srv", scatter_dimension=0, tiled=True
        ).astype(jnp.float32),
        lax.psum_scatter(
            spread_value.astype(jnp.bfloat16), "srv", scatter_dimension=0, tiled=True
        ).astype(jnp.float32),
    )
    return (attention, q_summed, k_summed.astype(jnp.bfloat16), v_summed.astype(jnp.bfloat16))


def solution(mesh):
    placed = (
        P("dp", "srv", "head"),
        P(("dp", "head"), None),
        P(("dp", "head"), None),
        P("dp", "srv", "head"),
        P("dp"),
    )
    return jax.shard_map(
        local,
        mesh=mesh,
        in_specs=placed,
        out_specs=(
            P("dp", "srv", "head"),
            P("dp", "srv", "head"),
            P(("dp", "head", "srv"), None),
            P(("dp", "head", "srv"), None),
        ),
        check_vma=False,
    )
```

profile of v0, /device:TPU:2, one launch (start us, length us, event | category | flops | bytes accessed | tf_op | source)
XLA Modules:
  0.0 651.0 jit_solution(6897663471784736279)
XLA Ops:
  7.2 1.5 copy.61
  9.5 9.2 %all-to-all-start = ((bf16[80,8,128]{2,0,1:T(8,128)(2,1)}), bf16[80,8,128]{2,0,1:T(8,128)(2,1)S(1)}, u32[]{:S(2)}, u32[]{:S(2)}) async-start(bf16[80,8,128]{2,0,1:T(8,128)(2,1)} %copy_bitcast_fusion.3), calls=%async_computation | async-start | bytes 327680 | tf_op jit(solution)/shard_map/all_to_all | solution.py:16
  18.7 1.6 copy_bitcast_fusion.2
  21.0 31.2 %all-gather.1 = s32[16,1,640]{2,1,0:T(1,128)S(1)} all-gather(s32[1,1,640]{2,1,0:T(1,128)S(1)} %reshape.364), channel_id=1, replica_groups=mesh['dp'=16,'head'=8,'srv'=4] {'dp'}, dimensions={0}, use_global_device_ids=true | all-gather | bytes 43520 | tf_op jit(solution)/shard_map/all_gather | solution.py:23
  52.8 33.4 %all-gather.5.cloned.1.call-done = bf16[2048,2,128]{2,0,1:T(8,128)(2,1)} async-done(((bf16[128,2,128]{2,0,1:T(8,128)(2,1)}), bf16[2048,2,128]{2,0,1:T(8,128)(2,1)}) %all-gather.5.cloned.1.call-update) | async-done | bytes 1048592 | tf_op jit(solution)/shard_map/all_gather | solution.py:29
  86.3 1.3 copy.66
  87.6 4.8 all-to-all-start.1
  92.4 7.6 %while.39 = (s32[]{:T(128)}, f32[4,512,2,1]{1,0,2,3:T(4,128)S(1)}, s32[4,512]{1,0:T(4,128)}, s32[640]{0:T(1024)S(1)}, s32[4,512]{1,0:T(4,128)S(1)}, /*index=5*/b...) while((s32[]{:T(128)}, f32[4,512,2,1]{1,0,2,3:T(4,128)S(1)}, ...), condition=%wide.region_2.3_spmd.clone, body=%wide.region_0.2_spmd.clone.sunk | while | flops 170720896 | bytes 1121917 | solution.py:64
  92.4 0.7 constant_dynamic-slice_fusion.12
  93.5 0.8 fusion.104
  94.3 0.7 constant_dynamic-slice_fusion.12
  95.4 0.8 fusion.104
  96.2 0.7 constant_dynamic-slice_fusion.12
  97.3 0.8 fusion.104
  99.2 0.8 fusion.104
  100.0 55.1 %pmax.7 = f32[2048,2,1]{0,1,2:T(2,128)} all-reduce(f32[2048,2,1]{0,1,2:T(2,128)S(1)} %reshape.354), channel_id=1, replica_groups=mesh['dp'=16,'head'=8,'srv'=4] {'dp'}, use_global_device_ids=true, to_apply=%region_3.4 | all-reduce | flops 4096 | bytes 32768 | tf_op jit(solution)/shard_map/pmax | solution.py:65
  155.1 22.3 %while.40 = (s32[]{:T(128)}, f32[4,512,2,128]{3,2,1,0:T(2,128)S(1)}, f32[4,512,2,1]{1,3,2,0:T(1,128)}, s32[4,512]{1,0:T(4,128)}, s32[640]{0:T(1024)S(1)}, /*inde...) while((s32[]{:T(128)}, ...), condition=%wide.region_6.7_spmd.clone, body=%wide.region_4.6_spmd.clone.sunk | while | flops 341769856 | bytes 8437397 | solution.py:89
  156.9 1.1 fusion.107
  157.9 1.7 fusion.108
  162.4 1.0 fusion.107
  163.5 1.7 fusion.108
  168.0 1.0 fusion.107
  169.1 1.7 fusion.108
  173.6 1.0 fusion.107
  174.6 1.7 fusion.108
  177.4 2.1 copy.88
  181.1 1.3 dynamic-slice
  183.0 63.6 %reduce-scatter.8.cloned.1.call-done = f32[128,2]{1,0:T(8,128)} async-done(((f32[2048,2]{1,0:T(8,128)}), f32[128,2]{1,0:T(8,128)}) %reduce-scatter.8.cloned.1.call-update) | async-done | bytes 1040
  246.6 0.9 copy.87
  248.3 27.4 %all_gather.17 = f32[2048,2,1]{0,1,2:T(2,128)S(1)} all-gather(f32[128,2,1]{0,1,2:T(2,128)S(1)} %log_add_fusion), channel_id=1, replica_groups=mesh['dp'=16,'head'=8,'srv'=4] {'dp'}, dimensions={0}, use_global_device_ids=true | all-gather | bytes 17408 | tf_op jit(solution)/shard_map/all_gather | solution.py:106
  275.7 115.2 %all-reduce.10.cloned.1.call-done = f32[2048,2,128]{2,1,0:T(2,128)} async-done(((f32[2048,2,128]{2,1,0:T(2,128)}), f32[2048,2,128]{2,1,0:T(2,128)}) %all-reduce.10.cloned.1.call-update) | async-done | bytes 2097168
  390.9 1.7 multiply_reduce_fusion
  392.6 35.8 %all-gather = f32[2048,2]{1,0:T(8,128)S(1)} all-gather(f32[128,2]{1,0:T(8,128)S(1)} %get-tuple-element.445), channel_id=2, replica_groups=mesh['dp'=16,'head'=8,'srv'=4] {'dp'}, dimensions={0}, use_global_device_ids=true | all-gather | bytes 17408 | tf_op jit(solution)/shard_map/all_gather | solution.py:107
  428.7 32.1 %all-gather.7.cloned.1.call-done = bf16[2048,2,128]{2,0,1:T(8,128)(2,1)} async-done(((bf16[128,2,128]{2,0,1:T(8,128)(2,1)}), bf16[2048,2,128]{2,0,1:T(8,128)(2,1)}) %all-gather.7.cloned.1.call-update) | async-done | bytes 1048592 | tf_op jit(solution)/shard_map/all_gather | solution.py:30
  460.8 37.4 %while.41 = (s32[]{:T(128)}, f32[640,1,128]{0,2,1:T(8,128)S(1)}, f32[640,1,128]{0,2,1:T(8,128)}, bf16[4,512,2,128]{3,1,2,0:T(8,128)(2,1)}, bf16[4,512,2,1,128]{4...) while((s32[]{:T(128)}, f32[640,1,128]{0,2,1:T(8,128)S(1)}, ...), condition=%wide.region_11.12_spmd.clone, body=%wide.region_10.11_spmd.clone.sunk | while | flops 846938752 | bytes 35077916 | solution.py:151
  461.4 0.8 constant_dynamic-slice_fusion.14
  462.5 2.0 fusion.120
  465.0 3.6 fusion.122
  469.2 1.0 copy-done.5
  470.7 0.8 constant_dynamic-slice_fusion.14
  471.8 2.0 fusion.120
  474.4 3.6 fusion.122
  478.5 1.0 copy-done.5
  480.1 0.8 constant_dynamic-slice_fusion.14
  481.1 2.0 fusion.120
  483.7 3.6 fusion.122
  487.9 1.0 copy-done.5
  489.4 0.8 constant_dynamic-slice_fusion.14
  490.5 2.0 fusion.120
  493.1 3.6 fusion.122
  497.2 1.0 copy-done.5
  498.2 0.8 copy.78
  499.0 4.9 all-to-all-start.2
  503.9 3.3 copy.77
  507.2 0.8 copy.80
  508.0 0.9 all-to-all-done.2
  508.9 4.8 all-to-all-start.3
  513.7 5.0 all-to-all-done.3
  518.8 12.6 %fusion.72 = (bf16[24,1024]{1,0:T(8,128)(2,1)S(1)}, bf16[24,1024]{1,0:T(8,128)(2,1)S(1)}) fusion(bf16[80,1024]{1,0:T(8,128)(2,1)S(1)} %copy_bitcast_fusion.1, bf16[80,1024]{1,0:T(8,128)(2,1)S(1)} %copy_bitcast_fusion), kind=kCustom, calls=%all-reduce-scatter.2 | all-reduce-scatter fusion | flops 196609 | bytes 428032
  531.4 1.6 collective-permute-start
  533.0 3.1 collective-permute-start.1
  536.0 1.3 dynamic-slice.10
  539.6 103.4 %all-reduce.12.cloned.1.call-done = bf16[2048,2,128]{2,1,0:T(2,128)(2,1)} async-done(((bf16[2048,2,128]{2,1,0:T(2,128)(2,1)}), bf16[2048,2,128]{2,1,0:T(2,128)(2,1)}) %all-reduce.12.cloned.1.call-update) | async-done | bytes 1048592
  643.0 1.5 constant_dynamic-slice_fusion.8
  (133 shorter events, 27.3 us)
Async XLA Ops:
  7.2 1.6 copy-start
  7.2 85.2 %copy-start.3 = (s32[640]{0:T(1024)S(1)}, s32[640]{0:T(1024)}, u32[]{:S(2)}) copy-start(s32[640]{0:T(1024)} %param.15) | copy-start | bytes 7684
  7.2 79.1 %all-gather.5.cloned.1.call-start = ((), (), s32[]{:S(2)}) async-start(), calls=%async_computation.5 | async-start | bytes 1114112 | tf_op jit(solution)/shard_map/all_gather | solution.py:29
  9.5 78.1 %all-to-all-start = ((bf16[80,8,128]{2,0,1:T(8,128)(2,1)}), bf16[80,8,128]{2,0,1:T(8,128)(2,1)S(1)}, u32[]{:S(2)}, u32[]{:S(2)}) async-start(bf16[80,8,128]{2,0,1:T(8,128)(2,1)} %copy_bitcast_fusion.3), calls=%async_computation | async-start | bytes 327680 | tf_op jit(solution)/shard_map/all_to_all | solution.py:16
  87.6 67.6 %all-to-all-start.1 = ((bf16[80,8,128]{2,0,1:T(8,128)(2,1)}), bf16[80,8,128]{2,0,1:T(8,128)(2,1)}, u32[]{:S(2)}, u32[]{:S(2)}) async-start(bf16[80,8,128]{2,0,1:T(8,128)(2,1)} %copy_bitcast_fusion.2), calls=%async_computation.1 | async-start | bytes 327680 | tf_op jit(solution)/shard_map/all_to_all | solution.py:17
  92.4 154.2 %reduce-scatter.8.cloned.1.call-start = ((), (), s32[]{:S(2)}) async-start(), calls=%async_computation.7 | async-start | bytes 1114112
  177.4 2.2 copy-start.2
  177.4 2.9 copy-start.7
  179.6 211.3 %all-reduce.10.cloned.1.call-start = ((), (), s32[]{:S(2)}) async-start(), calls=%async_computation.8 | async-start | bytes 4194304
  180.3 280.5 %all-gather.7.cloned.1.call-start = ((), (), s32[]{:S(2)}) async-start(), calls=%async_computation.6 | async-start | bytes 1114112 | tf_op jit(solution)/shard_map/all_gather | solution.py:30
  461.3 3.2 copy-start.1
  465.0 3.6 copy-start.4
  469.2 1.0 copy-start.5
  470.7 3.2 copy-start.1
  474.4 3.6 copy-start.4
  478.5 1.0 copy-start.5
  480.0 3.2 copy-start.1
  483.7 3.6 copy-start.4
  487.9 1.0 copy-start.5
  489.4 3.2 copy-start.1
  493.1 3.6 copy-start.4
  497.2 1.0 copy-start.5
  498.2 9.0 %copy-start.6 = (f32[640,1,128]{0,2,1:T(8,128)S(1)}, f32[640,1,128]{0,2,1:T(8,128)}, u32[]{:S(2)}) copy-start(f32[640,1,128]{0,2,1:T(8,128)} %get-tuple-element.183) | copy-start | bytes 983044
  499.0 9.9 %all-to-all-start.2 = ((bf16[8,80,128]{2,1,0:T(8,128)(2,1)}), bf16[8,80,128]{2,1,0:T(8,128)(2,1)S(1)}, u32[]{:S(2)}, u32[]{:S(2)}) async-start(bf16[8,80,128]{2,1,0:T(8,128)(2,1)} %bitcast.15), calls=%async_computation.2 | async-start | bytes 327680 | tf_op jit(solution)/shard_map/all_to_all | solution.py:161
  503.9 139.1 %all-reduce.12.cloned.1.call-start = ((), (), s32[]{:S(2)}) async-start(), calls=%async_computation.9 | async-start | bytes 2097152
  508.9 9.8 %all-to-all-start.3 = ((bf16[8,80,128]{2,1,0:T(8,128)(2,1)}), bf16[8,80,128]{2,1,0:T(8,128)(2,1)S(1)}, u32[]{:S(2)}, u32[]{:S(2)}) async-start(bf16[8,80,128]{2,1,0:T(8,128)(2,1)} %bitcast.17), calls=%async_computation.3 | async-start | bytes 327680 | tf_op jit(solution)/shard_map/all_to_all | solution.py:168
  531.4 6.6 %collective-permute-start = (bf16[12,1024]{1,0:T(8,128)(2,1)S(1)}, bf16[12,1024]{1,0:T(8,128)(2,1)S(1)}, u32[]{:S(2)}, u32[]{:S(2)}) collective-permute-start(bf16[12,1024]{1,0:T(8,128)(2,1)S(1)} %slice.16), channel_id=1, source_target_pairs={{0,1},{1,2},{2,3},{4,5},{5,6},{6,7},{8,9},{9,10},{10,11},{12,13},{... | collective-permute-start | bytes 73736
  533.0 5.2 collective-permute-start.1
Sparse Core Ops, SparseCore 0:
  10.7 75.5 all-gather.4
  179.7 66.8 reduce-scatter.7
  249.1 141.7 all-reduce.9
  393.6 67.1 all-gather.6
  507.3 135.5 all-reduce.11
where the time goes:
time: 653 us; the launch traced here: 651 us
  waiting for transfers between devices  354 us (54%)
  blocking collectives  162 us (25%)
  matrix products  42.8 us (7%)
  local copies, waits for them, and re-layouts  40.5 us (6%)
  starting transfers between devices  28.4 us (4%)
  between operations  15.3 us (2%)
  other arithmetic  7 us (1%)
    unnamed x10, waiting for transfers between devices  283 us
    pmax x1, blocking collectives, local(): row_max = lax.pmax(local_max.reshape(query_total, pair_heads, groups), 'dp')  55.1 us
    all_gather x1, blocking collectives, local(): lax.all_gather(delta_home, 'dp', axis=0, tiled=True)  35.8 us
    all_gather x1, waiting for transfers between devices, local(): lax.all_gather(queries, 'dp', axis=0, tiled=True)  33.4 us
    all_gather x1, waiting for transfers between devices, local(): lax.all_gather(output_gradient, 'dp', axis=0, tiled=True)  32.1 us
    all_gather x1, blocking collectives, local(): all_docs = lax.all_gather(doc_ids, 'dp', axis=0, tiled=True)  31.2 us
    all_gather x1, blocking collectives, local(): lax.all_gather(log_home, 'dp', axis=0, tiled=True)  27.4 us
    dot_general x4, matrix products, compute(): jnp.einsum('gjpk,pjgd->kgd', probs.astype(jnp.bfloat16), grad_block, pref...  14.3 us
  transfers between devices with their start and end apart: 11, of which 7 were waited for; matrix products, arithmetic and copies ran while one was open for 6% of the time, Pallas kernels for 0%

commit v1 on v0

--- a/solution.py
+++ b/solution.py
@@ -6,6 +6,27 @@
 
 HEAD_SIZE = 128
 NEGATIVE = -1e30
+
+
+def joined_along(parts, dim):
+    lengths = list(parts.shape[1:])
+    lengths[dim] *= parts.shape[0]
+    return jnp.moveaxis(parts, 0, dim).reshape(lengths)
+
+
+def doubled(value, axis):
+    size, mine = (lax.axis_size(axis), lax.axis_index(axis))
+    tiles, apart = (value[None], 1)
+    while apart < size:
+        other = lax.ppermute(tiles, axis, [(i, i ^ apart) for i in range(size)])
+        low = mine & apart == 0
+        tiles = jnp.concatenate([jnp.where(low, tiles, other), jnp.where(low, other, tiles)])
+        apart *= 2
+    return tiles
+
+
+def collect(x, axis, dim):
+    return joined_along(doubled(x, axis), dim)
 
 
 def local(queries, keys, values, output_gradient, doc_ids):
@@ -103,7 +124,7 @@
     )
     delta_home = jnp.sum(grad_home * attn_home.astype(jnp.float32), axis=-1)
     log_all, delta_all = (
-        lax.all_gather(log_home, "dp", axis=0, tiled=True),
+        collect(log_home, "dp", 0),
         lax.all_gather(delta_home, "dp", axis=0, tiled=True),
     )
     attention = attn_home.reshape(home_rows, pair_heads, group_width)

time: 653 us -> 653 us (level)
  blocking collectives: 162 us -> 135 us
  starting transfers between devices: 28.4 us -> 49.7 us
  waiting for transfers between devices: 354 us -> 361 us
    all_gather x1 -> x0, blocking collectives: 27.4 us -> none  [local(): lax.all_gather(log_home, 'dp', axis=0, tiled=True)]
    ppermute x0 -> x4, starting transfers between devices: none -> 21.4 us  [doubled(): other = lax.ppermute(tiles, axis, [(i, i ^ apart) for i in range(size)])]
    ppermute x0 -> x4, waiting for transfers between devices: none -> 12.2 us  [doubled(): other = lax.ppermute(tiles, axis, [(i, i ^ apart) for i in range(size)])]
  transfers between devices with their start and end apart: 11 -> 15, of which waited for: 7 -> 11; matrix products, arithmetic and copies ran while one was open for 6% -> 6% of each run, Pallas kernels for 0% -> 0%
where the time goes in v1:
time: 653 us; the launch traced here: 651 us
  waiting for transfers between devices  361 us (55%)
  blocking collectives  135 us (21%)
  starting transfers between devices  49.7 us (8%)
  matrix products  42.9 us (7%)
  local copies, waits for them, and re-layouts  40.4 us (6%)
  between operations  15.3 us (2%)
  other arithmetic  7.07 us (1%)
    unnamed x10, waiting for transfers between devices  277 us
    pmax x1, blocking collectives, local(): row_max = lax.pmax(local_max.reshape(query_total, pair_heads, groups), 'dp')  55.1 us
    all_gather x1, blocking collectives, local(): lax.all_gather(delta_home, 'dp', axis=0, tiled=True)  35.7 us
    all_gather x1, waiting for transfers between devices, local(): lax.all_gather(queries, 'dp', axis=0, tiled=True)  33.5 us
    all_gather x1, waiting for transfers between devices, local(): lax.all_gather(output_gradient, 'dp', axis=0, tiled=True)  32.2 us
    all_gather x1, blocking collectives, local(): all_docs = lax.all_gather(doc_ids, 'dp', axis=0, tiled=True)  31.2 us
    ppermute x4, starting transfers between devices, doubled(): other = lax.ppermute(tiles, axis, [(i, i ^ apart) for i in range(size)])  21.4 us
    dot_general x4, matrix products, compute(): jnp.einsum('gjpk,pjgd->kgd', probs.astype(jnp.bfloat16), grad_block, pref...  14.3 us
  transfers between devices with their start and end apart: 15, of which 11 were waited for; matrix products, arithmetic and copies ran while one was open for 6% of the time, Pallas kernels for 0%

profile of v1, /device:TPU:2, one launch (start us, length us, event | category | flops | bytes accessed | tf_op | source)
XLA Modules:
  0.0 651.2 jit_solution(15184315082875059079)
XLA Ops:
  7.2 1.5 copy.63
  9.5 9.2 %all-to-all-start = ((bf16[80,8,128]{2,0,1:T(8,128)(2,1)}), bf16[80,8,128]{2,0,1:T(8,128)(2,1)S(1)}, u32[]{:S(2)}, u32[]{:S(2)}) async-start(bf16[80,8,128]{2,0,1:T(8,128)(2,1)} %copy_bitcast_fusion.3), calls=%async_computation | async-start | bytes 327680 | tf_op jit(solution)/shard_map/all_to_all | solution.py:37
  18.7 1.6 copy_bitcast_fusion.2
  21.0 31.2 %all-gather.1 = s32[16,1,640]{2,1,0:T(1,128)S(1)} all-gather(s32[1,1,640]{2,1,0:T(1,128)S(1)} %reshape.360), channel_id=1, replica_groups=mesh['dp'=16,'head'=8,'srv'=4] {'dp'}, dimensions={0}, use_global_device_ids=true | all-gather | bytes 43520 | tf_op jit(solution)/shard_map/all_gather | solution.py:44
  52.8 33.5 %all-gather.5.cloned.1.call-done = bf16[2048,2,128]{2,0,1:T(8,128)(2,1)} async-done(((bf16[128,2,128]{2,0,1:T(8,128)(2,1)}), bf16[2048,2,128]{2,0,1:T(8,128)(2,1)}) %all-gather.5.cloned.1.call-update) | async-done | bytes 1048592 | tf_op jit(solution)/shard_map/all_gather | solution.py:50
  86.3 1.3 copy.68
  87.6 4.8 all-to-all-start.1
  92.4 7.6 %while.39 = (s32[]{:T(128)}, f32[4,512,2,1]{1,0,2,3:T(4,128)S(1)}, s32[4,512]{1,0:T(4,128)}, s32[640]{0:T(1024)S(1)}, s32[4,512]{1,0:T(4,128)S(1)}, /*index=5*/b...) while((s32[]{:T(128)}, f32[4,512,2,1]{1,0,2,3:T(4,128)S(1)}, ...), condition=%wide.region_2.3_spmd.clone, body=%wide.region_0.2_spmd.clone.sunk | while | flops 170720896 | bytes 1121917 | solution.py:85
  93.5 0.8 fusion.104
  95.4 0.8 fusion.104
  97.3 0.8 fusion.104
  99.2 0.8 fusion.104
  100.0 55.1 %pmax.7 = f32[2048,2,1]{0,1,2:T(2,128)} all-reduce(f32[2048,2,1]{0,1,2:T(2,128)S(1)} %reshape.351), channel_id=1, replica_groups=mesh['dp'=16,'head'=8,'srv'=4] {'dp'}, use_global_device_ids=true, to_apply=%region_3.4 | all-reduce | flops 4096 | bytes 32768 | tf_op jit(solution)/shard_map/pmax | solution.py:86
  155.2 22.3 %while.40 = (s32[]{:T(128)}, f32[4,512,2,128]{3,2,1,0:T(2,128)S(1)}, f32[4,512,2,1]{1,3,2,0:T(1,128)}, s32[4,512]{1,0:T(4,128)}, s32[640]{0:T(1024)S(1)}, /*inde...) while((s32[]{:T(128)}, ...), condition=%wide.region_6.7_spmd.clone, body=%wide.region_4.6_spmd.clone.sunk | while | flops 341769856 | bytes 8437397 | solution.py:110
  156.9 1.0 fusion.107
  158.0 1.7 fusion.108
  162.5 1.0 fusion.107
  163.5 1.7 fusion.108
  168.1 1.1 fusion.107
  169.1 1.7 fusion.108
  173.6 1.0 fusion.107
  174.7 1.7 fusion.108
  177.5 2.1 copy.91
  181.1 65.4 %reduce-scatter.8.cloned.1.call-done = f32[128,2]{1,0:T(8,128)} async-done(((f32[2048,2]{1,0:T(8,128)}), f32[128,2]{1,0:T(8,128)}) %reduce-scatter.8.cloned.1.call-update) | async-done | bytes 1040
  246.6 0.9 copy.90
  248.2 2.9 collective-permute-start
  251.1 2.5 collective-permute-done
  253.6 3.6 collective-permute-start.1
  257.2 2.8 collective-permute-done.1
  260.0 5.7 collective-permute-start.2
  265.8 3.8 collective-permute-done.2
  269.5 9.1 %collective-permute-start.3 = (f32[8,128,2,1]{1,2,3,0:T(2,128)S(1)}, f32[8,128,2,1]{1,2,3,0:T(2,128)S(1)}, u32[]{:S(2)}, u32[]{:S(2)}) collective-permute-start(f32[8,128,2,1]{1,2,3,0:T(2,128)S(1)} %pad_maximum_fusion.1), channel_id=1, source_target_pairs={{0,256},{32,288},{64,320},{96,352},{128,384},{160,416},{192,448},{... | collective-permute-start | bytes 24584 | tf_op jit(solution)/shard_map/ppermute | solution.py:21
  278.7 1.3 dynamic-slice
  280.7 3.2 collective-permute-done.3
  284.0 107.2 %all-reduce.10.cloned.1.call-done = f32[2048,2,128]{2,1,0:T(2,128)} async-done(((f32[2048,2,128]{2,1,0:T(2,128)}), f32[2048,2,128]{2,1,0:T(2,128)}) %all-reduce.10.cloned.1.call-update) | async-done | bytes 2097168
  391.1 1.7 multiply_reduce_fusion
  392.9 35.7 %all-gather = f32[2048,2]{1,0:T(8,128)S(1)} all-gather(f32[128,2]{1,0:T(8,128)S(1)} %get-tuple-element.445), channel_id=2, replica_groups=mesh['dp'=16,'head'=8,'srv'=4] {'dp'}, dimensions={0}, use_global_device_ids=true | all-gather | bytes 17408 | tf_op jit(solution)/shard_map/all_gather | solution.py:128
  428.9 32.2 %all-gather.7.cloned.1.call-done = bf16[2048,2,128]{2,0,1:T(8,128)(2,1)} async-done(((bf16[128,2,128]{2,0,1:T(8,128)(2,1)}), bf16[2048,2,128]{2,0,1:T(8,128)(2,1)}) %all-gather.7.cloned.1.call-update) | async-done | bytes 1048592 | tf_op jit(solution)/shard_map/all_gather | solution.py:51
  461.2 37.3 %while.41 = (s32[]{:T(128)}, f32[640,1,128]{0,2,1:T(8,128)S(1)}, f32[640,1,128]{0,2,1:T(8,128)}, bf16[4,512,2,128]{3,1,2,0:T(8,128)(2,1)}, bf16[4,512,2,1,128]{4...) while((s32[]{:T(128)}, f32[640,1,128]{0,2,1:T(8,128)S(1)}, ...), condition=%wide.region_11.12_spmd.clone, body=%wide.region_10.11_spmd.clone.sunk | while | flops 846938752 | bytes 35077916 | solution.py:172
  462.8 2.0 fusion.120
  465.4 3.6 fusion.122
  469.5 1.0 copy-done.5
  472.1 2.0 fusion.120
  474.7 3.6 fusion.122
  478.9 1.0 copy-done.5
  481.4 2.0 fusion.120
  484.0 3.6 fusion.122
  488.2 1.0 copy-done.5
  490.8 2.0 fusion.120
  493.4 3.6 fusion.122
  497.5 1.0 copy-done.5
  498.5 0.8 copy.81
  499.3 4.8 all-to-all-start.2
  504.1 3.3 copy.80
  507.5 0.8 copy.83
  508.3 0.9 all-to-all-done.2
  509.1 4.8 all-to-all-start.3
  513.9 5.0 all-to-all-done.3
  519.0 12.6 %fusion.72 = (bf16[24,1024]{1,0:T(8,128)(2,1)S(1)}, bf16[24,1024]{1,0:T(8,128)(2,1)S(1)}) fusion(bf16[80,1024]{1,0:T(8,128)(2,1)S(1)} %copy_bitcast_fusion.1, bf16[80,1024]{1,0:T(8,128)(2,1)S(1)} %copy_bitcast_fusion), kind=kCustom, calls=%all-reduce-scatter.2 | all-reduce-scatter fusion | flops 196609 | bytes 428032
  531.6 1.6 collective-permute-start.4
  533.2 3.1 collective-permute-start.5
  536.2 1.3 dynamic-slice.10
  539.8 103.3 %all-reduce.12.cloned.1.call-done = bf16[2048,2,128]{2,1,0:T(2,128)(2,1)} async-done(((bf16[2048,2,128]{2,1,0:T(2,128)(2,1)}), bf16[2048,2,128]{2,1,0:T(2,128)(2,1)}) %all-reduce.12.cloned.1.call-update) | async-done | bytes 1048592
  643.1 1.5 constant_dynamic-slice_fusion.8
  (148 shorter events, 32.5 us)
Async XLA Ops:
  7.2 1.6 copy-start
  7.2 85.2 %copy-start.3 = (s32[640]{0:T(1024)S(1)}, s32[640]{0:T(1024)}, u32[]{:S(2)}) copy-start(s32[640]{0:T(1024)} %param.15) | copy-start | bytes 7684
  7.2 79.1 %all-gather.5.cloned.1.call-start = ((), (), s32[]{:S(2)}) async-start(), calls=%async_computation.5 | async-start | bytes 1114112 | tf_op jit(solution)/shard_map/all_gather | solution.py:50
  9.5 78.1 %all-to-all-start = ((bf16[80,8,128]{2,0,1:T(8,128)(2,1)}), bf16[80,8,128]{2,0,1:T(8,128)(2,1)S(1)}, u32[]{:S(2)}, u32[]{:S(2)}) async-start(bf16[80,8,128]{2,0,1:T(8,128)(2,1)} %copy_bitcast_fusion.3), calls=%async_computation | async-start | bytes 327680 | tf_op jit(solution)/shard_map/all_to_all | solution.py:37
  87.6 67.6 %all-to-all-start.1 = ((bf16[80,8,128]{2,0,1:T(8,128)(2,1)}), bf16[80,8,128]{2,0,1:T(8,128)(2,1)}, u32[]{:S(2)}, u32[]{:S(2)}) async-start(bf16[80,8,128]{2,0,1:T(8,128)(2,1)} %copy_bitcast_fusion.2), calls=%async_computation.1 | async-start | bytes 327680 | tf_op jit(solution)/shard_map/all_to_all | solution.py:38
  92.4 154.2 %reduce-scatter.8.cloned.1.call-start = ((), (), s32[]{:S(2)}) async-start(), calls=%async_computation.7 | async-start | bytes 1114112
  177.5 2.2 copy-start.2
  177.5 2.9 copy-start.7
  179.6 211.5 %all-reduce.10.cloned.1.call-start = ((), (), s32[]{:S(2)}) async-start(), calls=%async_computation.8 | async-start | bytes 4194304
  180.4 280.8 %all-gather.7.cloned.1.call-start = ((), (), s32[]{:S(2)}) async-start(), calls=%async_computation.6 | async-start | bytes 1114112 | tf_op jit(solution)/shard_map/all_gather | solution.py:51
  248.2 5.5 collective-permute-start
  253.6 6.4 collective-permute-start.1
  260.0 9.5 %collective-permute-start.2 = (f32[4,128,2,1]{1,2,3,0:T(2,128)S(1)}, f32[4,128,2,1]{1,2,3,0:T(2,128)S(1)}, u32[]{:S(2)}, u32[]{:S(2)}) collective-permute-start(f32[4,128,2,1]{1,2,3,0:T(2,128)S(1)} %pad_maximum_fusion.2), channel_id=1, source_target_pairs={{0,128},{32,160},{64,192},{96,224},{128,0},{160,32},{192,64},{224,... | collective-permute-start | bytes 12296 | tf_op jit(solution)/shard_map/ppermute | solution.py:21
  269.5 14.4 %collective-permute-start.3 = (f32[8,128,2,1]{1,2,3,0:T(2,128)S(1)}, f32[8,128,2,1]{1,2,3,0:T(2,128)S(1)}, u32[]{:S(2)}, u32[]{:S(2)}) collective-permute-start(f32[8,128,2,1]{1,2,3,0:T(2,128)S(1)} %pad_maximum_fusion.1), channel_id=1, source_target_pairs={{0,256},{32,288},{64,320},{96,352},{128,384},{160,416},{192,448},{... | collective-permute-start | bytes 24584 | tf_op jit(solution)/shard_map/ppermute | solution.py:21
  461.7 3.2 copy-start.1
  465.4 3.6 copy-start.4
  469.5 1.0 copy-start.5
  471.0 3.2 copy-start.1
  474.7 3.6 copy-start.4
  478.8 1.0 copy-start.5
  480.3 3.2 copy-start.1
  484.0 3.6 copy-start.4
  488.2 1.0 copy-start.5
  489.7 3.2 copy-start.1
  493.4 3.6 copy-start.4
  497.5 1.0 copy-start.5
  498.5 8.9 %copy-start.6 = (f32[640,1,128]{0,2,1:T(8,128)S(1)}, f32[640,1,128]{0,2,1:T(8,128)}, u32[]{:S(2)}) copy-start(f32[640,1,128]{0,2,1:T(8,128)} %get-tuple-element.183) | copy-start | bytes 983044
  499.3 9.8 %all-to-all-start.2 = ((bf16[8,80,128]{2,1,0:T(8,128)(2,1)}), bf16[8,80,128]{2,1,0:T(8,128)(2,1)S(1)}, u32[]{:S(2)}, u32[]{:S(2)}) async-start(bf16[8,80,128]{2,1,0:T(8,128)(2,1)} %bitcast.16), calls=%async_computation.2 | async-start | bytes 327680 | tf_op jit(solution)/shard_map/all_to_all | solution.py:182
  504.1 139.0 %all-reduce.12.cloned.1.call-start = ((), (), s32[]{:S(2)}) async-start(), calls=%async_computation.9 | async-start | bytes 2097152
  509.1 9.8 %all-to-all-start.3 = ((bf16[8,80,128]{2,1,0:T(8,128)(2,1)}), bf16[8,80,128]{2,1,0:T(8,128)(2,1)S(1)}, u32[]{:S(2)}, u32[]{:S(2)}) async-start(bf16[8,80,128]{2,1,0:T(8,128)(2,1)} %bitcast.18), calls=%async_computation.3 | async-start | bytes 327680 | tf_op jit(solution)/shard_map/all_to_all | solution.py:189
  531.6 6.6 %collective-permute-start.4 = (bf16[12,1024]{1,0:T(8,128)(2,1)S(1)}, bf16[12,1024]{1,0:T(8,128)(2,1)S(1)}, u32[]{:S(2)}, u32[]{:S(2)}) collective-permute-start(bf16[12,1024]{1,0:T(8,128)(2,1)S(1)} %slice.16), channel_id=1, source_target_pairs={{0,1},{1,2},{2,3},{4,5},{5,6},{6,7},{8,9},{9,10},{10,11},{12,13},{... | collective-permute-start | bytes 73736
  533.2 5.2 collective-permute-start.5
Sparse Core Ops, SparseCore 0:
  10.7 75.5 all-gather.4
  179.8 66.7 reduce-scatter.7
  249.0 142.0 all-reduce.9
  393.9 67.2 all-gather.6
  507.6 135.5 all-reduce.11
